TPU v7x, 128 devices: a whole 4x4x4 slice. The times are simulated.
128 devices in a mesh: ep: 32 (over x, z, core), hp: 4 (over y).
Axes of the slice: x: 4, y: 4, z: 4, core: 2. Of those that a mesh axis runs over, the one named last changes fastest.
Arguments:
- tokens: bfloat16 [8192, 4096], P('ep'), may hold values from -6 to 6
- expert_rows: int32 [64, 512], P('ep'), may hold values from 0 to 8191, as said below
- expert_counts: int32 [64], P('ep'), may hold values from 0 to 512, as said below
- choice_gates: float32 [64, 512], P('ep'), may hold values from 0.05 to 1
- gate_proj: bfloat16 [64, 4096, 1536], P('ep', None, 'hp'), may hold values from -0.09375 to 0.09375
- up_proj: bfloat16 [64, 4096, 1536], P('ep', None, 'hp'), may hold values from -0.09375 to 0.09375
- down_proj: bfloat16 [64, 1536, 4096], P('ep', 'hp'), may hold values from -0.15625 to 0.15625
Outputs:
- combined: bfloat16 [8192, 4096], P('ep', 'hp')
Inputs may be any that keep to these rules, and one draw needn't show every extreme that they name: `expert_rows`: the first expert_counts[e] entries of row e are distinct tokens; later entries are padding and may name any token. Among the valid entries of one expert at most 16 lie in the 256 tokens of one index of ep, and in every draw some expert has exactly 16 from every index of ep. `expert_counts`: some expert's count is exactly 512 in every draw.
All inputs are finite; a program needn't handle non-finite values.
Results may differ from a plain program's by a relative error of at most 0.0049.
Values may be sent and summed in bfloat16 or wider, within the bound.
A program may use at most 128 MiB of HBM per device.

v0:
```python
import jax
import jax.numpy as jnp
from jax import lax
from jax.sharding import PartitionSpec as P


def per_device(tokens, expert_rows, expert_counts, choice_gates, gate_proj, up_proj, down_proj):
    groups = lax.axis_size("ep")
    member = lax.axis_index("ep")
    tok_rows = tokens.shape[0]
    features = tokens.shape[1]
    local_experts = expert_rows.shape[0]
    capacity = expert_rows.shape[1]
    bucket = capacity // groups
    all_rows, all_counts = (
        lax.all_gather(expert_rows, "ep", axis=0, tiled=True),
        lax.all_gather(expert_counts, "ep", axis=0, tiled=True),
    )
    ordered = jnp.transpose(all_rows.reshape(groups, local_experts, capacity), (1, 0, 2))
    counted = jnp.transpose(all_counts.reshape(groups, local_experts), (1, 0))
    positions = jnp.arange(capacity, dtype=jnp.int32)
    is_valid = positions[None, None, :] < counted[:, :, None]
    offset = ordered - member * tok_rows
    is_mine = is_valid & (offset >= 0) & (offset < tok_rows)
    rank_in = jnp.cumsum(is_mine.astype(jnp.int32), axis=2) - 1
    target = jnp.arange(bucket, dtype=jnp.int32)
    select = is_mine[:, :, None, :] & (rank_in[:, :, None, :] == target[None, None, :, None])
    picked = jnp.sum(jnp.where(select, offset[:, :, None, :], 0), axis=3)
    is_live = jnp.any(select, axis=3)
    taken = jnp.take(tokens, picked.reshape(-1), axis=0).reshape(
        local_experts, groups, bucket, features
    )
    outgoing = jnp.where(is_live[..., None], taken, jnp.zeros((), tokens.dtype))
    own_valid = positions[None, :] < expert_counts[:, None]
    source = expert_rows // tok_rows
    from_peer = own_valid[:, :, None] & (
        source[:, :, None] == jnp.arange(groups, dtype=jnp.int32)[None, None, :]
    )
    within = jnp.sum(
        jnp.where(from_peer, jnp.cumsum(from_peer.astype(jnp.int32), axis=1) - 1, 0), axis=2
    )
    slot_of = source * bucket + within
    spread = own_valid[:, :, None] & (slot_of[:, :, None] == positions[None, None, :])
    bucket_gate = jnp.sum(jnp.where(spread, choice_gates[:, :, None], 0.0), axis=1)
    arrived = lax.all_to_all(outgoing, "ep", split_axis=1, concat_axis=1, tiled=True).reshape(
        local_experts, capacity, features
    )
    gate_act = jnp.einsum("ecd,edh->ech", arrived, gate_proj, preferred_element_type=jnp.float32)
    up_act = jnp.einsum("ecd,edh->ech", arrived, up_proj, preferred_element_type=jnp.float32)
    hidden = (jax.nn.silu(gate_act) * up_act).astype(jnp.bfloat16)
    partial_value = jnp.einsum(
        "ech,ehd->ecd", hidden, down_proj, preferred_element_type=jnp.float32
    )
    partial_value = partial_value * bucket_gate[:, :, None]
    live_flat = is_live.reshape(-1)[:, None]
    picked_flat = picked.reshape(-1)
    returned = lax.all_to_all(
        partial_value.reshape(local_experts, groups, bucket, features),
        "ep",
        split_axis=1,
        concat_axis=1,
        tiled=True,
    )
    values = jnp.where(live_flat, returned.reshape(-1, features), 0.0)
    summed = jnp.zeros((tok_rows, features), jnp.float32).at[picked_flat].add(values)
    combined = lax.psum_scatter(summed, "hp", scatter_dimension=1, tiled=True)
    return combined.astype(jnp.bfloat16)


def solution(mesh):
    return jax.shard_map(
        per_device,
        mesh=mesh,
        in_specs=(
            P("ep", None),
            P("ep", None),
            P("ep"),
            P("ep", None),
            P("ep", None, "hp"),
            P("ep", None, "hp"),
            P("ep", "hp", None),
        ),
        out_specs=P("ep", "hp"),
        check_vma=False,
    )
```

profile of v0, /device:TPU:1, one launch (start us, length us, event | category | flops | bytes accessed | tf_op | source)
XLA Modules:
  0.0 619.9 jit_solution(8733204039383797310)
XLA Ops:
  6.5 1.4 dynamic-slice
  8.6 0.9 dynamic-update-slice
  9.4 15.5 %all-reduce = s32[64]{0:T(128)S(1)} all-reduce(s32[64]{0:T(128)S(1)} %dynamic-update-slice), channel_id=1, replica_groups=mesh['ep'=32,'hp'=4] {'ep'}, use_global_device_ids=true, to_apply=%add | all-reduce | flops 64 | bytes 512
  24.9 0.1 reshape.130
  25.0 25.8 %all-gather = s32[32,2,512]{2,1,0:T(2,128)S(1)} all-gather(s32[1,2,512]{2,1,0:T(2,128)} %bitcast.44), channel_id=1, replica_groups=mesh['ep'=32,'hp'=4] {'ep'}, dimensions={0}, use_global_device_ids=true | all-gather | bytes 135168 | tf_op jit(solution)/shard_map/all_gather | solution.py:16
  50.8 0.2 fusion.13
  51.0 0.1 reshape.138
  51.2 2.3 reduce-window.14
  53.5 0.3 slice_reduce_fusion.1
  53.9 0.1 copy_bitcast_fusion
  54.1 1.2 fusion.4
  55.2 1.2 select_reduce_fusion.1
  56.6 7.7 %gather_fusion = bf16[1024,4096]{1,0:T(8,128)(2,1)} fusion(bf16[256,4096]{1,0:T(8,128)(2,1)S(1)} %copy-done, s32[1024]{0:T(1024)S(1)} %broadcast_clamp_fusion), kind=kCustom, calls=%fused_computation | custom fusion | bytes 16781312 | tf_op jit(solution)/shard_map/jit(_take)/gather | solution.py:30
  64.4 7.4 %fusion = bf16[2,32,16,4096]{3,2,0,1:T(8,128)(2,1)} fusion(bf16[2,32,16,4096]{3,2,1,0:T(8,128)(2,1)} %bitcast.39, pred[2,32,16]{2,0,1:T(4,128)(4,1)S(1)} %copy.42, pred[2,32,16]{2,0,1:T(4,128)(4,1)S(1)} %copy.41), kind=kLoop, calls=%fused_computation.5 | loop fusion | flops 8388608 | bytes 16779264 | tf_op jit(solution)/shard_map/jit(_where)/select_n | solution.py:33
  71.8 5.4 all-to-all-start
  77.4 2.3 reduce-window.16
  79.7 0.3 slice_reduce_fusion
  80.2 0.1 fusion.8
  80.3 0.6 select_reduce_fusion
  80.9 103.8 %all-to-all-done = bf16[2,32,16,4096]{3,2,0,1:T(8,128)(2,1)} async-done(((bf16[2,32,16,4096]{3,2,0,1:T(8,128)(2,1)}), bf16[2,32,16,4096]{3,2,0,1:T(8,128)(2,1)}, u32[]{:S(2)}, u32[]{:S(2)}) %all-to-all-start) | async-done | bytes 8388640 | tf_op jit(solution)/shard_map/all_to_all | solution.py:45
  184.7 7.7 %copy.44 = bf16[2,32,16,4096]{3,2,1,0:T(8,128)(2,1)} copy(bf16[2,32,16,4096]{3,2,0,1:T(8,128)(2,1)} %all-to-all-done) | data formatting | bytes 16777216 | tf_op jit(solution)/shard_map/all_to_all | solution.py:45
  192.4 8.8 %fusion.14 = f32[2,512,384]{2,1,0:T(8,128)S(1)} fusion(bf16[2,512,4096]{2,1,0:T(8,128)(2,1)} %bitcast.41, bf16[2,4096,384]{2,1,0:T(8,128)(2,1)} %param.11), kind=kOutput, calls=%fused_computation.46 | convolution fusion | flops 3221225472 | bytes 16252928 | tf_op jit(solution)/shard_map/ecd,edh->ech/dot_general | solution.py:48
  201.2 16.3 %convolution_multiply_fusion = f32[2,512,4096]{2,1,0:T(8,128)} fusion(bf16[2,384,4096]{2,1,0:T(8,128)(2,1)} %param.13, f32[2,512]{1,0:T(2,128)S(1)} %select_reduce_fusion, f32[2,512,384]{2,1,0:T(8,128)S(1)} %fusion.14, bf16[2,512,4096]{2,1,0:T(8,128)(2,1)} %bitcast.42, bf16[2,4096,384]{2,1,0:T(8,128)(2,1)} %param.12), kind=kOutput, calls=%fused_computation.3 | convolution fusion | flops 6449004544 | bytes 39325696 | tf_op jit(solution)/shard_map/ech,ehd->ecd/dot_general | solution.py:51
  217.5 11.6 %copy.46 = f32[2,32,16,4096]{3,2,0,1:T(8,128)} copy(f32[2,32,16,4096]{3,2,1,0:T(8,128)} %bitcast.40) | data formatting | bytes 33554432 | tf_op jit(solution)/shard_map/reshape | solution.py:58
  229.1 22.7 %all-to-all-start.1 = ((f32[2,32,16,4096]{3,2,0,1:T(8,128)}), f32[2,32,16,4096]{3,2,0,1:T(8,128)}, u32[]{:S(2)}, u32[]{:S(2)}) async-start(f32[2,32,16,4096]{3,2,0,1:T(8,128)} %copy.46), calls=%async_computation.1 | async-start | bytes 33554432 | tf_op jit(solution)/shard_map/all_to_all | solution.py:57
  251.9 0.1 broadcast_in_dim.88
  251.9 231.0 %all-to-all-done.1 = f32[2,32,16,4096]{3,2,0,1:T(8,128)} async-done(((f32[2,32,16,4096]{3,2,0,1:T(8,128)}), f32[2,32,16,4096]{3,2,0,1:T(8,128)}, u32[]{:S(2)}, u32[]{:S(2)}) %all-to-all-start.1) | async-done | bytes 16777248 | tf_op jit(solution)/shard_map/all_to_all | solution.py:57
  483.0 6.7 %copy.47 = f32[2,32,16,4096]{3,2,1,0:T(8,128)S(1)} copy(f32[2,32,16,4096]{3,2,0,1:T(8,128)} %all-to-all-done.1) | data formatting | bytes 33554432 | tf_op jit(solution)/shard_map/all_to_all | solution.py:57
  489.7 7.5 %bitcast_select_fusion = f32[1024,4096]{1,0:T(8,128)} fusion(f32[2,32,16,4096]{3,2,1,0:T(8,128)S(1)} %copy.47, pred[1024]{0:T(1024)(128)(4,1)S(1)} %broadcast_in_dim.88), kind=kLoop, calls=%fused_computation.2 | loop fusion | flops 4194304 | bytes 33555456 | tf_op jit(solution)/shard_map/jit(_where)/select_n | solution.py:64
  497.2 28.5 %scatter_custom_fusion = f32[256,4096]{1,0:T(8,128)} fusion(s32[1024]{0:T(1024)S(1)} %bitcast.46, f32[1024,4096]{1,0:T(8,128)} %bitcast_select_fusion, f32[]{:T(128)} %constant.33.clone.1), kind=kCustom, calls=%fused_computation.10 | custom fusion | flops 4194304 | bytes 4194816 | tf_op jit(solution)/shard_map/scatter-add | solution.py:65
  525.7 85.2 %reduce-scatter.2.cloned.1.call-done = f32[256,1024]{1,0:T(8,128)} async-done(((f32[256,4096]{1,0:T(8,128)}), f32[256,1024]{1,0:T(8,128)}) %reduce-scatter.2.cloned.1.call-update) | async-done | bytes 1048592 | tf_op jit(solution)/shard_map/reduce_scatter | solution.py:66
  610.9 2.1 convert_element_type.14
  (33 shorter events, 0.6 us)
Async XLA Ops:
  6.5 50.1 %copy-start = (bf16[256,4096]{1,0:T(8,128)(2,1)S(1)}, bf16[256,4096]{1,0:T(8,128)(2,1)}, u32[]{:S(2)}) copy-start(bf16[256,4096]{1,0:T(8,128)(2,1)} %param.7) | copy-start | bytes 6291460
  71.8 5.5 copy-start.2
  71.8 5.5 copy-start.4
  71.8 8.5 %copy-start.3 = (f32[2,512]{1,0:T(2,128)S(1)}, f32[2,512]{1,0:T(2,128)}, u32[]{:S(2)}) copy-start(f32[2,512]{1,0:T(2,128)} %param.10) | copy-start | bytes 12292
  71.8 112.9 %all-to-all-start = ((bf16[2,32,16,4096]{3,2,0,1:T(8,128)(2,1)}), bf16[2,32,16,4096]{3,2,0,1:T(8,128)(2,1)}, u32[]{:S(2)}, u32[]{:S(2)}) async-start(bf16[2,32,16,4096]{3,2,0,1:T(8,128)(2,1)} %fusion), calls=%async_computation | async-start | bytes 16777216 | tf_op jit(solution)/shard_map/all_to_all | solution.py:45
  229.1 253.9 %all-to-all-start.1 = ((f32[2,32,16,4096]{3,2,0,1:T(8,128)}), f32[2,32,16,4096]{3,2,0,1:T(8,128)}, u32[]{:S(2)}, u32[]{:S(2)}) async-start(f32[2,32,16,4096]{3,2,0,1:T(8,128)} %copy.46), calls=%async_computation.1 | async-start | bytes 33554432 | tf_op jit(solution)/shard_map/all_to_all | solution.py:57
  251.8 359.1 %reduce-scatter.2.cloned.1.call-start = ((), (), s32[]{:S(2)}) async-start(), calls=%async_computation.3 | async-start | bytes 5242880 | tf_op jit(solution)/shard_map/reduce_scatter | solution.py:66
  489.7 123.4 %copy-start.1 = (bf16[256,4096]{1,0:T(8,128)(2,1)S(1)}, bf16[256,4096]{1,0:T(8,128)(2,1)}, u32[]{:S(2)}) copy-start(bf16[256,4096]{1,0:T(8,128)(2,1)} %param.7) | copy-start | bytes 6291460
Sparse Core Ops, SparseCore 0:
  525.8 85.0 reduce-scatter.1
where the time goes:
time: 620 us
  waiting for transfers between devices  420 us (68%)
  other arithmetic  53.8 us (9%)
  blocking collectives  41.3 us (7%)
  local copies, waits for them, and re-layouts  37.1 us (6%)
  starting transfers between devices  28.2 us (5%)
  matrix products  25.1 us (4%)
  between operations  14.3 us (2%)
    all_to_all x1, waiting for transfers between devices, per_device(): lax.all_to_all(partial_value.reshape(local_experts, groups, bucket, featu...  231 us
    all_to_all x1, waiting for transfers between devices, per_device(): lax.all_to_all(outgoing, 'ep', split_axis=1, concat_axis=1, tiled=True)  104 us
    reduce_scatter x1, waiting for transfers between devices, per_device(): combined = lax.psum_scatter(summed, 'hp', scatter_dimension=1, tiled=True)  85.2 us
    scatter-add x1, other arithmetic, per_device(): jnp.zeros((tok_rows, features), jnp.float32).at[picked_flat].add(values)  28.5 us
    all_gather x1, blocking collectives, per_device(): lax.all_gather(expert_rows, 'ep', axis=0, tiled=True)  25.8 us
    all_to_all x1, starting transfers between devices, per_device(): lax.all_to_all(partial_value.reshape(local_experts, groups, bucket, featu...  22.7 us
    dot_general x1, matrix products, per_device(): jnp.einsum('ech,ehd->ecd', hidden, down_proj, preferred_element_type=jnp....  16.3 us
    unnamed x1, blocking collectives  15.5 us
  transfers between devices with their start and end apart: 3, of which 3 were waited for; matrix products, arithmetic and copies ran while one was open for 1% of the time, Pallas kernels for 0%

commit v1 on v0

v1 whole, which is shorter than its diff:
```python
import functools

import jax
import jax.numpy as jnp
from jax import lax
from jax.experimental import pallas as pl
from jax.experimental.pallas import tpu as pltpu
from jax.sharding import PartitionSpec as P

MESH = pl.DeviceIdType.MESH
SLOT = 16
BF16, F32, I32 = jnp.bfloat16, jnp.float32, jnp.int32


def plan(groups):
    side = {32: 4, 8: 2}[groups]
    ring = [min(d, side - d) for d in range(side)]
    chips = sorted(
        ((dx, dz) for dx in range(side) for dz in range(side)),
        key=lambda c: (side > 2 and 2 in c, ring[c[0]] + ring[c[1]], c[0] != c[1], c),
    )
    offsets = [(dx, dz, dc) for dx, dz in chips for dc in range(2)]
    if groups == 32:
        chunks = {
            "z": (0, 2, True), "a": (2, 10, True), "b": (10, 18, True), "d": (18, 22, True),
            "t": (22, 28, False), "s": (28, 32, False),
        }
        sends = "sztbda"
        schedule = (
            "XsXzXtCzEzGsXbGt",
            "AzBzTzFsFtXdCsEs",
            "XaCtEtAsBsCbEbAt",
            "BtTsCdEdTtAbBbCa",
            "EaAdBdTbAaBaTdMs",
            "MtMbTaMzMdMa",
        )
    else:
        chunks = {"a": (0, 4, True), "s": (4, 8, False)}
        sends = "sa"
        schedule = ("XsXaGsCaFs", "EaAaBaCs", "EsTaAsBsTs", "MaMs")
    steps = [(part[i], part[i + 1]) for part in schedule for i in range(0, len(part), 2)]
    return side, offsets, chunks, sends, steps


def kernel(
    groups, lanes_hp,
    rows_ref, counts_ref, gates_ref, tok_hbm, gate_hbm, up_hbm, down_hbm,
    out_ref,
    tok, wgu, wd, chosen, pout, via, fin, back, ret, onehot, acc, picks_out, picks_in, gate_col,
    w_sem, pick_s, pick_r, disp_s, disp_r, ret_s, ret_r, y_s, y_r,
):
    side, offsets, chunks, sends, schedule = plan(groups)
    places = groups
    n_exp, cap = rows_ref.shape
    n_q, n_tok, feat = tok.shape
    hid = wd.shape[2]
    me = lax.axis_index("ep")
    y = lax.axis_index("hp")
    mx, mz, mc = me // (side * 2), (me // 2) % side, me % 2
    y_up, y_dn, y_far = (y + 1) % n_q, (y + n_q - 1) % n_q, (y + 2) % n_q

    def shifted(p, sign):
        dx, dz, dc = offsets[p]
        px = (mx + (sign * dx) % side) % side
        pz = (mz + (sign * dz) % side) % side
        return (px * side + pz) * 2 + (mc + dc) % 2

    def expert_of(p):
        return {"ep": shifted(p, 1)}

    def owner_of(p):
        return {"ep": shifted(p, -1)}

    def remote(src, dst, s_sem, r_sem, device):
        return pltpu.make_async_remote_copy(
            src_ref=src, dst_ref=dst, send_sem=s_sem, recv_sem=r_sem,
            device_id=device, device_id_type=MESH,
        )

    loads = []

    def load(src, dst):
        copy = pltpu.make_async_copy(src, dst, w_sem.at[len(loads)])
        copy.start()
        loads.append(copy)

    for q in range(n_q):
        load(tok_hbm.at[:, pl.ds(q * feat, feat)], tok.at[q])
    for e in range(n_exp):
        load(gate_hbm.at[e], wgu.at[e, :, pl.ds(0, hid)])
        load(up_hbm.at[e], wgu.at[e, :, pl.ds(hid, hid)])
        for q in range(n_q):
            load(down_hbm.at[e, :, pl.ds(q * feat, feat)], wd.at[e, q])

    barrier = pltpu.get_barrier_semaphore()
    for p in range(1, places):
        pl.semaphore_signal(barrier, inc=1, device_id=expert_of(p), device_id_type=MESH)
    for target in (y_up, y_dn):
        pl.semaphore_signal(barrier, inc=1, device_id={"hp": target}, device_id_type=MESH)

    listed = rows_ref[...]
    entry = lax.broadcasted_iota(I32, (1, cap), 1)
    log_side = side.bit_length() - 1
    log_tok = n_tok.bit_length() - 1
    source = lax.shift_right_logical(listed, log_tok)
    row_in = listed & (n_tok - 1)
    sx = lax.shift_right_logical(source, log_side + 1)
    sz = lax.shift_right_logical(source, 1) & (side - 1)
    sc = source & 1
    code = (((mx - sx) & (side - 1)) * side + ((mz - sz) & (side - 1))) * 2 + ((mc - sc) & 1)
    place_code = [(dx * side + dz) * 2 + dc for dx, dz, dc in offsets]
    before = (
        lax.broadcasted_iota(I32, (cap, cap), 0) < lax.broadcasted_iota(I32, (cap, cap), 1)
    ).astype(F32).astype(BF16)
    place_id = lax.broadcasted_iota(I32, (places, 1), 0)
    place_codes = sum(jnp.where(place_id == p, c, 0) for p, c in enumerate(place_code))
    for e in range(n_exp):
        own_code = jnp.where(entry < counts_ref[e], code[e : e + 1, :], -1)
        hit = (own_code == place_codes).astype(F32)
        rank = jnp.dot(hit.astype(BF16), before, preferred_element_type=F32)
        slot = jnp.sum(
            hit * (rank + (lax.broadcasted_iota(I32, (places, cap), 0) * SLOT + 1).astype(F32)),
            axis=0, keepdims=True,
        ) - 1.0
        row_e = row_in[e : e + 1, :].astype(F32) + 1.0
        gate_e = gates_ref[e : e + 1, :]
        block = 4 * SLOT
        for b in range(places * SLOT // block):
            ids = (lax.broadcasted_iota(I32, (block, cap), 0) + b * block).astype(F32)
            here = ids == slot
            pick = jnp.sum(jnp.where(here, row_e, 0.0), axis=1, keepdims=True) - 1.0
            gate = jnp.sum(jnp.where(here, gate_e, 0.0), axis=1, keepdims=True)
            wide = jnp.broadcast_to(pick, (block, 128)).astype(BF16)
            picks_out[e, 4 * b : 4 * b + 4] = wide.reshape(4, SLOT, 128)
            gate_col[e, b * block : (b + 1) * block] = jnp.broadcast_to(gate, (block, 128))
    picks_in[:, 0] = picks_out[:, 0]

    pl.semaphore_wait(barrier, places - 1 + 2)

    order = [p for name in sends for p in range(*chunks[name][:2])]
    picks = {}
    for p in order:
        if p:
            picks[p] = remote(
                picks_out.at[:, p], picks_in.at[:, p], pick_s.at[p], pick_r.at[p], owner_of(p)
            )
            picks[p].start()

    for copy in loads[:n_q]:
        copy.wait()

    out_going = {}
    sem_ids = iter(range(y_s.shape[0]))
    started = []

    def send_y(src, dst, target):
        k = next(sem_ids)
        copy = remote(src, dst, y_s.at[k], y_r.at[k], {"hp": target})
        copy.start()
        started.append(copy)
        return copy

    state = {}
    returns = {}
    weights_ready = False

    for step, name in schedule:
        lo, hi, whole = chunks[name]
        n, m = hi - lo, (hi - lo) * SLOT
        rng = pl.ds(lo, n)
        if step == "X":
            for p in range(lo, hi):
                if p:
                    picks[p].wait_recv()
            token_id = lax.broadcasted_iota(I32, (m, 128), 1).astype(F32)
            for e in range(n_exp):
                want = picks_in[e, lo:hi].reshape(m, 128).astype(F32)
                parts = [
                    (token_id + float(128 * k) == want).astype(F32) for k in range(n_tok // 128)
                ]
                hot = jnp.concatenate(parts, axis=1).astype(BF16)
                onehot[e, lo:hi] = hot.reshape(n, SLOT, n_tok)

                def rows_of(q):
                    taken = jnp.dot(hot, tok[q], preferred_element_type=F32).astype(BF16)
                    pout[q, e, lo:hi] = taken.reshape(n, SLOT, feat)
                    if lo == 0:
                        chosen[q, e, 0] = taken[:SLOT]

                if whole:
                    pl.loop(0, n_q)(rows_of)
                else:
                    rows_of(y)
            for p in range(lo, hi):
                if p:
                    at = (slice(None), slice(None), p) if whole else (y, slice(None), p)
                    out_going[p] = remote(
                        pout.at[at], chosen.at[at], disp_s.at[p], disp_r.at[p], expert_of(p)
                    )
                    out_going[p].start()
        elif step == "G":
            for p in range(lo, hi):
                out_going[p].wait_recv()
            state[name, "G"] = [
                send_y(chosen.at[y, :, rng], chosen.at[y, :, rng], target) for target in (y_up, y_dn)
            ]
        elif step == "F":
            for copy in state[name, "G"]:
                copy.wait_recv()
            state[name, "F"] = [
                send_y(chosen.at[y_dn, 0, rng], chosen.at[y_dn, 0, rng], y_up),
                send_y(chosen.at[y_up, 1, rng], chosen.at[y_up, 1, rng], y_dn),
            ]
        elif step in "CE":
            e = "CE".index(step)
            if e == 0:
                for p in range(lo, hi):
                    if p and whole:
                        out_going[p].wait_recv()
                for p in range(lo, hi):
                    if p:
                        out_going[p].wait_send()
            if not weights_ready:
                for copy in loads[n_q:]:
                    copy.wait()
                weights_ready = True
            if not whole:
                state[name, "F"][e].wait_recv()
            total = jnp.zeros((m, 2 * hid), F32)
            for q in range(n_q):
                total += jnp.dot(
                    chosen[q, e, lo:hi].reshape(m, feat),
                    wgu[e, q * feat : (q + 1) * feat, :],
                    preferred_element_type=F32,
                )
            gate, up = total[:, :hid], total[:, hid:]
            hidden = (gate / (1.0 + jnp.exp(-gate)) * up).astype(BF16)
            weight = gate_col[e, lo * SLOT : hi * SLOT][:, :1]

            @pl.loop(0, n_q)
            def _(q):
                value = jnp.dot(hidden, wd[e, q], preferred_element_type=F32) * weight
                pout[q, e, lo:hi] = value.astype(BF16).reshape(n, SLOT, feat)

            ahead, behind = (y_up, y_dn) if e == 0 else (y_dn, y_up)
            state[name, "V", e] = send_y(pout.at[y_far, e, rng], via.at[e, rng], ahead)
            state[name, "D", e] = send_y(pout.at[behind, e, rng], fin.at[1 - e, e, rng], behind)
        elif step in "AB":
            e = "AB".index(step)
            ahead = (y_up, y_dn)[e]
            state[name, "V", e].wait_recv()
            pout[ahead, e, lo:hi] = (
                pout[ahead, e, lo:hi].astype(F32) + via[e, lo:hi].astype(F32)
            ).astype(BF16)
            state[name, "S", e] = send_y(pout.at[ahead, e, rng], fin.at[e, e, rng], ahead)
        elif step == "T":
            for e in range(n_exp):
                state[name, "D", e].wait_recv()
                state[name, "S", e].wait_recv()
                back[e, lo:hi] = (
                    pout[y, e, lo:hi].astype(F32)
                    + fin[0, e, lo:hi].astype(F32)
                    + fin[1, e, lo:hi].astype(F32)
                ).astype(BF16)
            for p in range(lo, hi):
                if p:
                    returns[p] = remote(
                        back.at[:, p], ret.at[:, p], ret_s.at[p], ret_r.at[p], owner_of(p)
                    )
                    returns[p].start()
                else:
                    ret[:, 0] = back[:, 0]
        else:
            for p in range(lo, hi):
                if p:
                    returns[p].wait_recv()
            total = None
            for e in range(n_exp):
                value = lax.dot_general(
                    onehot[e, lo:hi].reshape(m, n_tok),
                    ret[e, lo:hi].reshape(m, feat),
                    (((0,), (0,)), ((), ())),
                    preferred_element_type=F32,
                )
                total = value if total is None else total + value
            merged = [w for s, w in schedule if s == "M"]
            if name != merged[0]:
                total = total + acc[...]
            if name == merged[-1]:
                out_ref[...] = total.astype(BF16)
            else:
                acc[...] = total

    for copy in [*picks.values(), *returns.values(), *started]:
        copy.wait_send()


def per_device(tokens, expert_rows, expert_counts, choice_gates, gate_proj, up_proj, down_proj):
    groups = lax.axis_size("ep")
    n_q = lax.axis_size("hp")
    n_tok, width = tokens.shape
    n_exp, cap = expert_rows.shape
    hid = gate_proj.shape[2]
    feat = width // n_q
    chunks = plan(groups)[2]
    hops = sum(6 if whole else 10 for _, _, whole in chunks.values())
    any_space = pl.BlockSpec(memory_space=pl.ANY)
    vmem = pl.BlockSpec(memory_space=pltpu.VMEM)
    dma = pltpu.SemaphoreType.DMA
    full = (n_q, n_exp, groups, SLOT, feat)
    return pl.pallas_call(
        functools.partial(kernel, groups, n_q),
        out_shape=jax.ShapeDtypeStruct((n_tok, feat), BF16),
        in_specs=[vmem, pl.BlockSpec(memory_space=pltpu.SMEM), vmem, any_space, any_space, any_space, any_space],
        out_specs=vmem,
        scratch_shapes=[
            pltpu.VMEM((n_q, n_tok, feat), BF16),
            pltpu.VMEM((n_exp, width, 2 * hid), BF16),
            pltpu.VMEM((n_exp, n_q, hid, feat), BF16),
            pltpu.VMEM(full, BF16),
            pltpu.VMEM(full, BF16),
            pltpu.VMEM((2, groups, SLOT, feat), BF16),
            pltpu.VMEM((2, n_exp, groups, SLOT, feat), BF16),
            pltpu.VMEM((n_exp, groups, SLOT, feat), BF16),
            pltpu.VMEM((n_exp, groups, SLOT, feat), BF16),
            pltpu.VMEM((n_exp, groups, SLOT, n_tok), BF16),
            pltpu.VMEM((n_tok, feat), F32),
            pltpu.VMEM((n_exp, groups, SLOT, 128), BF16),
            pltpu.VMEM((n_exp, groups, SLOT, 128), BF16),
            pltpu.VMEM((n_exp, groups * SLOT, 128), F32),
            dma((n_q + n_exp * (2 + n_q),)),
            dma((groups,)),
            dma((groups,)),
            dma((groups,)),
            dma((groups,)),
            dma((groups,)),
            dma((groups,)),
            dma((hops,)),
            dma((hops,)),
        ],
        compiler_params=pltpu.CompilerParams(
            collective_id=0, has_side_effects=True, vmem_limit_bytes=60 * 1024 * 1024
        ),
        cost_estimate=pl.CostEstimate(
            flops=6 * n_exp * cap * width * hid, bytes_accessed=24 * 1024 * 1024, transcendentals=0
        ),
    )(
        expert_rows, expert_counts, choice_gates,
        tokens, gate_proj, up_proj, down_proj,
    )


def solution(mesh):
    return jax.shard_map(
        per_device,
        mesh=mesh,
        in_specs=(
            P("ep", None),
            P("ep", None),
            P("ep"),
            P("ep", None),
            P("ep", None, "hp"),
            P("ep", None, "hp"),
            P("ep", "hp", None),
        ),
        out_specs=P("ep", "hp"),
        check_vma=False,
    )
```

time: 620 us -> 129 us (0.21)
  waiting for transfers between devices: 420 us -> 0 us
  Pallas kernels: 0 us -> 127 us
  other arithmetic: 53.8 us -> 0 us
  blocking collectives: 41.3 us -> 0 us
  local copies, waits for them, and re-layouts: 37.1 us -> 1.87 us
  starting transfers between devices: 28.2 us -> 0 us
  matrix products: 25.1 us -> 0 us
  between operations: 14.3 us -> 0.01 us
    all_to_all x2 -> x0, waiting for transfers between devices: 335 us -> none  [the longest x1 231 us: per_device(): lax.all_to_all(partial_value.reshape(local_experts, groups, bucket, featu...]
    pallas_call x0 -> x1, Pallas kernels: none -> 127 us  [per_device(): pl.pallas_call(functools.partial(kernel, groups, n_q), out_shape=jax.Shap...]
    reduce_scatter x1 -> x0, waiting for transfers between devices: 85.2 us -> none  [per_device(): combined = lax.psum_scatter(summed, 'hp', scatter_dimension=1, tiled=True)]
    scatter-add x1 -> x0, other arithmetic: 28.5 us -> none  [per_device(): jnp.zeros((tok_rows, features), jnp.float32).at[picked_flat].add(values)]
    all_to_all x2 -> x0, starting transfers between devices: 28.1 us -> none  [the longest x1 22.7 us: per_device(): lax.all_to_all(partial_value.reshape(local_experts, groups, bucket, featu...]
    all_gather x1 -> x0, blocking collectives: 25.8 us -> none  [per_device(): lax.all_gather(expert_rows, 'ep', axis=0, tiled=True)]
    dot_general x2 -> x0, matrix products: 25.1 us -> none  [the longest x1 16.3 us: per_device(): jnp.einsum('ech,ehd->ecd', hidden, down_proj, preferred_element_type=jnp....]
    unnamed x1 -> x0, blocking collectives: 15.5 us -> none
  transfers between devices with their start and end apart: 3 -> 0, of which waited for: 3 -> 0; matrix products, arithmetic and copies ran while one was open for 1% -> 0% of each run, Pallas kernels for 0% -> 0%
where the time goes in v1:
time: 129 us; the launch traced here: 128 us
  Pallas kernels  127 us (98%)
  local copies, waits for them, and re-layouts  1.87 us (1%)
    pallas_call x1, Pallas kernels, per_device(): pl.pallas_call(functools.partial(kernel, groups, n_q), out_shape=jax.Shap...  127 us

profile of v1, /device:TPU:1, one launch (start us, length us, event | category | flops | bytes accessed | tf_op | source)
XLA Modules:
  0.0 128.4 jit_solution(17181938755092011910)
XLA Ops:
  0.0 126.5 %shard_map.73 = bf16[256,1024]{1,0:T(8,128)(2,1)} custom-call(s32[2,512]{1,0:T(2,128)} %rows_ref.1, s32[2]{0:T(128)} %counts_ref.1, f32[2,512]{1,0:T(2,128)} %gates_ref.1, bf16[256,4096]{1,0:T(8,128)(2,1)} %tok_hbm.1, bf16[2,4096,384]{2,1,0:T(8,128)(2,1)} %gate_hbm.1, bf16[2,4096,384]{2,1,0:T(8,128)(2,1)} %up_hbm.1, bf16[2,384,4096]{2,1,0:T(8,128)(2,1)} %down_hbm.1), custom_call_target="tpu_custom_call" | custom-call | flops 9663676416 | bytes 25165824 | tf_op jit(solution)/shard_map/pallas_call | solution.py:311
  126.5 1.9 %copy.9 = bf16[256,1024]{1,0:T(8,128)(2,1)} copy(bf16[256,1024]{1,0:T(8,128)(2,1)} %shard_map.73) | data formatting | bytes 1048576

commit v2 on v1

--- a/solution.py
+++ b/solution.py
@@ -22,17 +22,18 @@
     offsets = [(dx, dz, dc) for dx, dz in chips for dc in range(2)]
     if groups == 32:
         chunks = {
-            "z": (0, 2, True), "a": (2, 10, True), "b": (10, 18, True), "d": (18, 22, True),
-            "t": (22, 28, False), "s": (28, 32, False),
+            "z": (0, 2, True), "a": (2, 6, True), "e": (6, 10, True), "b": (10, 18, True),
+            "d": (18, 22, True), "t": (22, 28, False), "s": (28, 32, False),
         }
-        sends = "sztbda"
+        sends = "sztbdae"
         schedule = (
-            "XsXzXtCzEzGsXbGt",
-            "AzBzTzFsFtXdCsEs",
-            "XaCtEtAsBsCbEbAt",
-            "BtTsCdEdTtAbBbCa",
-            "EaAdBdTbAaBaTdMs",
-            "MtMbTaMzMdMa",
+            "XsXzXtCzEzGsXbAz",
+            "BzGtFsXdFtCsEsXa",
+            "XeTzCtEtAsBsCbEb",
+            "AtBtTsCdEdTtAbBb",
+            "CaEaAdBdTbCeEeAa",
+            "BaTdAeBeTaMsMtMb",
+            "TeMzMdMaMe",
         )
     else:
         chunks = {"a": (0, 4, True), "s": (4, 8, False)}

time: 129 us -> 127 us (0.984)
  Pallas kernels: 127 us -> 125 us
where the time goes in v2:
time: 127 us
  Pallas kernels  125 us (98%)
  local copies, waits for them, and re-layouts  1.87 us (1%)
    pallas_call x1, Pallas kernels, per_device(): pl.pallas_call(functools.partial(kernel, groups, n_q), out_shape=jax.Shap...  125 us

profile of v2, /device:TPU:1, one launch (start us, length us, event | category | flops | bytes accessed | tf_op | source)
XLA Modules:
  0.0 127.1 jit_solution(14750345754867467530)
XLA Ops:
  0.0 125.3 %shard_map.73 = bf16[256,1024]{1,0:T(8,128)(2,1)} custom-call(s32[2,512]{1,0:T(2,128)} %rows_ref.1, s32[2]{0:T(128)} %counts_ref.1, f32[2,512]{1,0:T(2,128)} %gates_ref.1, bf16[256,4096]{1,0:T(8,128)(2,1)} %tok_hbm.1, bf16[2,4096,384]{2,1,0:T(8,128)(2,1)} %gate_hbm.1, bf16[2,4096,384]{2,1,0:T(8,128)(2,1)} %up_hbm.1, bf16[2,384,4096]{2,1,0:T(8,128)(2,1)} %down_hbm.1), custom_call_target="tpu_custom_call" | custom-call | flops 9663676416 | bytes 25165824 | tf_op jit(solution)/shard_map/pallas_call | solution.py:312
  125.3 1.9 %copy.9 = bf16[256,1024]{1,0:T(8,128)(2,1)} copy(bf16[256,1024]{1,0:T(8,128)(2,1)} %shard_map.73) | data formatting | bytes 1048576
